TPU v7x, 512 devices: a whole 4x8x8 slice. The times are simulated.
512 devices in a mesh: row: 8 (over y), col: 16 (over x_lo, z), layer: 4 (over x_hi, core).
Axes of the slice: x: 4 (x_hi: 2, x_lo: 2; x = x_hi * 2 + x_lo), y: 8, z: 8, core: 2. Of those that a mesh axis runs over, the one named last changes fastest.
Arguments:
- integrals: bfloat16 [64, 1024, 3072], P('layer', 'col', 'row'), may hold values from -0.0234375 to 0.0234375
- amplitudes: bfloat16 [64, 1024, 2048], P('layer', 'row', 'col'), may hold values from -6 to 6
- coulomb: bfloat16 [3072, 2048], P(('row', 'layer'), 'col'), may hold values from -6 to 6
- row_gap: float32 [3072], P(('row', 'layer')), may hold values from 0.5 to 4
- col_gap: float32 [2048], P('col'), may hold values from 0.5 to 4
Outputs:
- residual: float32 [3072, 2048], P(('row', 'layer'), 'col')
All inputs are finite; a program needn't handle non-finite values.
Results may differ from a plain program's by a relative error of at most 0.0003.
Values may be sent and summed in bfloat16 or wider, within the bound.
No kernel may reach another device: no remote copies, remote signals or barrier semaphores. Data moves between devices by JAX's collectives and lax.ppermute only.
A program may use at most 64 MiB of HBM per device.

v0:
```python
import jax
import jax.numpy as jnp
from jax import lax
from jax.sharding import PartitionSpec as P


def local(integrals, amplitudes, coulomb, row_gap, col_gap):
    contract = (((0, 1), (0, 1)), ((), ()))
    gathered = lax.all_gather(amplitudes, "row", axis=1, tiled=True)
    partial_sum = lax.dot_general(
        lax.all_gather(integrals, "col", axis=1, tiled=True),
        gathered,
        contract,
        preferred_element_type=jnp.float32,
    )
    share_rows = coulomb.shape[0]
    summed_all = lax.psum(partial_sum, "layer")
    own_rows = lax.dynamic_slice_in_dim(
        summed_all, lax.axis_index("layer") * share_rows, share_rows, 0
    )
    gap_sum = row_gap[:, None] + col_gap[None, :]
    return (coulomb.astype(jnp.float32) + own_rows) / gap_sum


def solution(mesh):
    placed = (
        P("layer", "col", "row"),
        P("layer", "row", "col"),
        P(("row", "layer"), "col"),
        P(("row", "layer")),
        P("col"),
    )
    return jax.shard_map(
        local, mesh=mesh, in_specs=placed, out_specs=P(("row", "layer"), "col"), check_vma=False
    )
```

profile of v0, /device:TPU:1, one launch (start us, length us, event | category | flops | bytes accessed | tf_op | source)
XLA Modules:
  0.0 286.8 jit_solution(3546155924513565021)
XLA Ops:
  6.5 0.0 copy-start
  6.5 0.0 copy-start.1
  6.5 0.0 copy-start.2
  6.5 0.0 all-gather.5.cloned.1.call-start
  6.5 0.7 all-gather.5.cloned.1.call-update
  7.3 0.0 all-gather.3.cloned.1.call-start
  7.3 0.7 all-gather.3.cloned.1.call-update
  8.0 0.0 all-reduce.2.cloned.1.call-start
  8.1 64.0 %all-gather.5.cloned.1.call-done = bf16[16,1024,128]{2,1,0:T(8,128)(2,1)} async-done(((bf16[16,128,128]{2,1,0:T(8,128)(2,1)}), bf16[16,1024,128]{2,1,0:T(8,128)(2,1)}) %all-gather.5.cloned.1.call-update) | async-done | bytes 4194320 | tf_op jit(solution)/shard_map/all_gather | solution.py:9
  72.1 147.7 %all-gather.3.cloned.1.call-done = bf16[16,1024,384]{2,1,0:T(8,128)(2,1)} async-done(((bf16[16,64,384]{2,1,0:T(8,128)(2,1)}), bf16[16,1024,384]{2,1,0:T(8,128)(2,1)}) %all-gather.3.cloned.1.call-update) | async-done | bytes 12582928 | tf_op jit(solution)/shard_map/all_gather | solution.py:11
  219.8 9.9 %convolution_bitcast_fusion = f32[384,128]{1,0:T(8,128)} fusion(bf16[16,1024,384]{2,1,0:T(8,128)(2,1)} %all-gather.3.cloned.1.call-done, bf16[16,1024,128]{2,1,0:T(8,128)(2,1)} %all-gather.5.cloned.1.call-done), kind=kOutput, calls=%fused_computation | convolution fusion | flops 1610612736 | bytes 16973824 | tf_op jit(solution)/shard_map/dot_general | solution.py:10
  229.7 0.0 all-reduce.2.cloned.1.call-update
  229.7 49.0 %all-reduce.2.cloned.1.call-done = f32[384,128]{1,0:T(8,128)} async-done(((f32[384,128]{1,0:T(8,128)}), f32[384,128]{1,0:T(8,128)}) %all-reduce.2.cloned.1.call-update) | async-done | bytes 196624 | tf_op jit(solution)/shard_map/psum | solution.py:17
  278.7 0.0 copy-done
  278.7 0.0 copy-done.1
  278.7 0.0 copy-done.2
  278.7 1.5 add_divide_fusion
Async XLA Ops:
  6.5 272.2 %copy-start = (bf16[96,128]{1,0:T(8,128)(2,1)S(1)}, bf16[96,128]{1,0:T(8,128)(2,1)}, u32[]{:S(2)}) copy-start(bf16[96,128]{1,0:T(8,128)(2,1)} %param.7) | copy-start | bytes 73732
  6.5 272.2 %copy-start.1 = (f32[128]{0:T(128)S(1)}, f32[128]{0:T(128)}, u32[]{:S(2)}) copy-start(f32[128]{0:T(128)} %param.9) | copy-start | bytes 1540
  6.5 272.2 %copy-start.2 = (f32[96]{0:T(128)S(1)}, f32[96]{0:T(128)}, u32[]{:S(2)}) copy-start(f32[96]{0:T(128)} %param.8) | copy-start | bytes 1156
  6.5 65.6 %all-gather.5.cloned.1.call-start = ((), (), s32[]{:S(2)}) async-start(), calls=%async_computation.1 | async-start | bytes 4718592 | tf_op jit(solution)/shard_map/all_gather | solution.py:9
  7.3 212.5 %all-gather.3.cloned.1.call-start = ((), (), s32[]{:S(2)}) async-start(), calls=%async_computation | async-start | bytes 13369344 | tf_op jit(solution)/shard_map/all_gather | solution.py:11
  8.0 270.7 %all-reduce.2.cloned.1.call-start = ((), (), s32[]{:S(2)}) async-start(), calls=%async_computation.2 | async-start | bytes 393216 | tf_op jit(solution)/shard_map/psum | solution.py:17
Sparse Core Ops, SparseCore 0:
  9.4 62.6 all-gather.4
  74.2 145.5 all-gather.2
  229.8 48.8 all-reduce.1
where the time goes:
time: 287 us
  waiting for transfers between devices  262 us (91%)
  between operations  13.1 us (5%)
  matrix products  9.89 us (3%)
    all_gather x1, waiting for transfers between devices, local(): lax.all_gather(integrals, 'col', axis=1, tiled=True)  148 us
    all_gather x1, waiting for transfers between devices, local(): gathered = lax.all_gather(amplitudes, 'row', axis=1, tiled=True)  64 us
    psum x1, waiting for transfers between devices, local(): summed_all = lax.psum(partial_sum, 'layer')  49 us
    dot_general x1, matrix products, local(): lax.dot_general(lax.all_gather(integrals, 'col', axis=1, tiled=True), gat...  9.89 us
  transfers between devices with their start and end apart: 3, of which 3 were waited for; matrix products, arithmetic and copies ran while one was open for 0% of the time, Pallas kernels for 0%

commit v1 on v0

--- a/solution.py
+++ b/solution.py
@@ -14,7 +14,7 @@
         preferred_element_type=jnp.float32,
     )
     share_rows = coulomb.shape[0]
-    summed_all = lax.psum(partial_sum, "layer")
+    summed_all = jnp.sum(lax.all_gather(partial_sum, "layer"), axis=0)
     own_rows = lax.dynamic_slice_in_dim(
         summed_all, lax.axis_index("layer") * share_rows, share_rows, 0
     )

time: 287 us -> 247 us (0.86)
  waiting for transfers between devices: 262 us -> 213 us
  blocking collectives: 0 us -> 10.3 us
    psum x1 -> x0, waiting for transfers between devices: 49 us -> none  [local(): summed_all = lax.psum(partial_sum, 'layer')]
    all_gather x0 -> x1, blocking collectives: none -> 10.3 us  [local(): summed_all = jnp.sum(lax.all_gather(partial_sum, 'layer'), axis=0)]
  transfers between devices with their start and end apart: 3 -> 2, of which waited for: 3 -> 2; matrix products, arithmetic and copies ran while one was open for 0% -> 0% of each run, Pallas kernels for 0% -> 0%
where the time goes in v1:
time: 247 us
  waiting for transfers between devices  213 us (86%)
  between operations  13.4 us (5%)
  blocking collectives  10.3 us (4%)
  matrix products  9.2 us (4%)
    all_gather x1, waiting for transfers between devices, local(): lax.all_gather(integrals, 'col', axis=1, tiled=True)  148 us
    all_gather x1, waiting for transfers between devices, local(): gathered = lax.all_gather(amplitudes, 'row', axis=1, tiled=True)  64.1 us
    all_gather x1, blocking collectives, local(): summed_all = jnp.sum(lax.all_gather(partial_sum, 'layer'), axis=0)  10.3 us
    dot_general x1, matrix products, local(): lax.dot_general(lax.all_gather(integrals, 'col', axis=1, tiled=True), gat...  9.2 us
  transfers between devices with their start and end apart: 2, of which 2 were waited for; matrix products, arithmetic and copies ran while one was open for 0% of the time, Pallas kernels for 0%

profile of v1, /device:TPU:1, one launch (start us, length us, event | category | flops | bytes accessed | tf_op | source)
XLA Modules:
  0.0 247.0 jit_solution(3858858910519761225)
XLA Ops:
  6.5 0.0 copy-start
  6.5 0.0 copy-start.1
  6.5 0.0 copy-start.2
  6.5 0.0 all-gather.6.cloned.1.call-start
  6.5 0.7 all-gather.6.cloned.1.call-update
  7.3 0.0 all-gather.4.cloned.1.call-start
  7.3 0.7 all-gather.4.cloned.1.call-update
  8.0 64.1 %all-gather.6.cloned.1.call-done = bf16[16,1024,128]{2,1,0:T(8,128)(2,1)} async-done(((bf16[16,128,128]{2,1,0:T(8,128)(2,1)}), bf16[16,1024,128]{2,1,0:T(8,128)(2,1)}) %all-gather.6.cloned.1.call-update) | async-done | bytes 4194320 | tf_op jit(solution)/shard_map/all_gather | solution.py:9
  72.1 147.7 %all-gather.4.cloned.1.call-done = bf16[16,1024,384]{2,1,0:T(8,128)(2,1)} async-done(((bf16[16,64,384]{2,1,0:T(8,128)(2,1)}), bf16[16,1024,384]{2,1,0:T(8,128)(2,1)}) %all-gather.4.cloned.1.call-update) | async-done | bytes 12582928 | tf_op jit(solution)/shard_map/all_gather | solution.py:11
  219.8 9.2 %convolution_bitcast_fusion = f32[384,128]{1,0:T(8,128)S(1)} fusion(bf16[16,1024,384]{2,1,0:T(8,128)(2,1)} %all-gather.4.cloned.1.call-done, bf16[16,1024,128]{2,1,0:T(8,128)(2,1)} %all-gather.6.cloned.1.call-done), kind=kOutput, calls=%fused_computation | convolution fusion | flops 1610612736 | bytes 16973824 | tf_op jit(solution)/shard_map/dot_general | solution.py:10
  229.0 10.3 %all-gather = f32[1536,128]{1,0:T(8,128)S(1)} all-gather(f32[384,128]{1,0:T(8,128)S(1)} %convolution_bitcast_fusion), channel_id=2, replica_groups=mesh['row'=8,'col'=16,'layer'=4] {'layer'}, dimensions={0}, use_global_device_ids=true | all-gather | bytes 983040 | tf_op jit(solution)/shard_map/all_gather | solution.py:17
  239.4 0.0 copy-done
  239.4 0.0 copy-done.1
  239.4 0.0 copy-done.2
  239.4 0.7 add_divide_fusion
  (1 shorter events, 0.0 us)
Async XLA Ops:
  6.5 232.8 %copy-start = (bf16[96,128]{1,0:T(8,128)(2,1)S(1)}, bf16[96,128]{1,0:T(8,128)(2,1)}, u32[]{:S(2)}) copy-start(bf16[96,128]{1,0:T(8,128)(2,1)} %param.7) | copy-start | bytes 73732
  6.5 232.9 %copy-start.1 = (f32[128]{0:T(128)S(1)}, f32[128]{0:T(128)}, u32[]{:S(2)}) copy-start(f32[128]{0:T(128)} %param.9) | copy-start | bytes 1540
  6.5 232.9 %copy-start.2 = (f32[96]{0:T(128)S(1)}, f32[96]{0:T(128)}, u32[]{:S(2)}) copy-start(f32[96]{0:T(128)} %param.8) | copy-start | bytes 1156
  6.5 65.6 %all-gather.6.cloned.1.call-start = ((), (), s32[]{:S(2)}) async-start(), calls=%async_computation.1 | async-start | bytes 4718592 | tf_op jit(solution)/shard_map/all_gather | solution.py:9
  7.3 212.5 %all-gather.4.cloned.1.call-start = ((), (), s32[]{:S(2)}) async-start(), calls=%async_computation | async-start | bytes 13369344 | tf_op jit(solution)/shard_map/all_gather | solution.py:11
Sparse Core Ops, SparseCore 0:
  9.4 62.6 all-gather.5
  74.2 145.5 all-gather.3

commit v2 on v0

--- a/solution.py
+++ b/solution.py
@@ -8,7 +8,9 @@
     contract = (((0, 1), (0, 1)), ((), ()))
     gathered = lax.all_gather(amplitudes, "row", axis=1, tiled=True)
     partial_sum = lax.dot_general(
-        lax.all_gather(integrals, "col", axis=1, tiled=True),
+        jnp.concatenate(
+            lax.all_to_all(jnp.stack([integrals] * lax.axis_size("col")), "col", 0, 0), axis=1
+        ),
         gathered,
         contract,
         preferred_element_type=jnp.float32,

time: 287 us -> 396 us (1.38)
  waiting for transfers between devices: 262 us -> 340 us
  local copies, waits for them, and re-layouts: 0.01 us -> 18.5 us
  starting transfers between devices: 0.08 us -> 12 us
    all_to_all x0 -> x1, waiting for transfers between devices: none -> 278 us  [local(): lax.all_to_all(jnp.stack([integrals] * lax.axis_size('col')), 'col', 0, 0)]
    all_gather x1 -> x0, waiting for transfers between devices: 148 us -> none  [local(): lax.all_gather(integrals, 'col', axis=1, tiled=True)]
    all_gather x1, waiting for transfers between devices: 64 us -> 0.02 us  [local(): gathered = lax.all_gather(amplitudes, 'row', axis=1, tiled=True)]
    psum x1, waiting for transfers between devices: 49 us -> 61.4 us  [local(): summed_all = lax.psum(partial_sum, 'layer')]
    all_to_all x0 -> x1, starting transfers between devices: none -> 11.9 us  [local(): lax.all_to_all(jnp.stack([integrals] * lax.axis_size('col')), 'col', 0, 0)]
    all_to_all x0 -> x1, local copies, waits for them, and re-layouts: none -> 10.8 us  [local(): lax.all_to_all(jnp.stack([integrals] * lax.axis_size('col')), 'col', 0, 0)]
    another operation x0 -> x1, local copies, waits for them, and re-layouts: none -> 7.74 us  [local(): jnp.stack([integrals] * lax.axis_size('col'))]
  transfers between devices with their start and end apart: 3 -> 3, of which waited for: 3 -> 2; matrix products, arithmetic and copies ran while one was open for 0% -> 3% of each run, Pallas kernels for 0% -> 0%
where the time goes in v2:
time: 396 us
  waiting for transfers between devices  340 us (86%)
  local copies, waits for them, and re-layouts  18.5 us (5%)
  between operations  13.4 us (3%)
  starting transfers between devices  12 us (3%)
  matrix products  9.89 us (2%)
    all_to_all x1, waiting for transfers between devices, local(): lax.all_to_all(jnp.stack([integrals] * lax.axis_size('col')), 'col', 0, 0)  278 us
    psum x1, waiting for transfers between devices, local(): summed_all = lax.psum(partial_sum, 'layer')  61.4 us
    all_to_all x1, starting transfers between devices, local(): lax.all_to_all(jnp.stack([integrals] * lax.axis_size('col')), 'col', 0, 0)  11.9 us
    all_to_all x1, local copies, waits for them, and re-layouts, local(): lax.all_to_all(jnp.stack([integrals] * lax.axis_size('col')), 'col', 0, 0)  10.8 us
    dot_general x1, matrix products, local(): lax.dot_general(jnp.concatenate(lax.all_to_all(jnp.stack([integrals] * la...  9.89 us
  transfers between devices with their start and end apart: 3, of which 2 were waited for; matrix products, arithmetic and copies ran while one was open for 3% of the time, Pallas kernels for 0%

profile of v2, /device:TPU:1, one launch (start us, length us, event | category | flops | bytes accessed | tf_op | source)
XLA Modules:
  0.0 395.8 jit_solution(7481548405916938383)
XLA Ops:
  6.5 7.7 %stack.2 = bf16[16,16,64,384]{3,2,1,0:T(8,128)(2,1)} broadcast(bf16[16,64,384]{2,1,0:T(8,128)(2,1)} %param.5), dimensions={1,2,3} | broadcast | bytes 13369344 | tf_op jit(solution)/shard_map/stack | solution.py:12
  14.3 11.9 %all-to-all-start = ((bf16[16,16,64,384]{3,2,1,0:T(8,128)(2,1)}), bf16[16,16,64,384]{3,2,1,0:T(8,128)(2,1)}, u32[]{:S(2)}, u32[]{:S(2)}) async-start(bf16[16,16,64,384]{3,2,1,0:T(8,128)(2,1)} %stack.2), calls=%async_computation | async-start | bytes 25165824 | tf_op jit(solution)/shard_map/all_to_all | solution.py:12
  26.2 0.0 all-gather.2.cloned.1.call-start
  26.3 0.7 all-gather.2.cloned.1.call-update
  27.0 0.0 all-reduce.2.cloned.1.call-start
  27.0 278.3 %all-to-all-done = bf16[16,16,64,384]{3,2,1,0:T(8,128)(2,1)} async-done(((bf16[16,16,64,384]{3,2,1,0:T(8,128)(2,1)}), bf16[16,16,64,384]{3,2,1,0:T(8,128)(2,1)}, u32[]{:S(2)}, u32[]{:S(2)}) %all-to-all-start) | async-done | bytes 12582944 | tf_op jit(solution)/shard_map/all_to_all | solution.py:12
  305.3 10.8 %copy.8 = bf16[16,16,64,384]{3,2,0,1:T(8,128)(2,1)} copy(bf16[16,16,64,384]{3,2,1,0:T(8,128)(2,1)} %all-to-all-done) | data formatting | bytes 25165824 | tf_op jit(solution)/shard_map/all_to_all | solution.py:12
  316.1 0.0 copy-start
  316.1 0.0 copy-start.1
  316.1 0.0 copy-start.2
  316.1 0.0 all-gather.2.cloned.1.call-done
  316.1 9.9 %convolution_bitcast_fusion = f32[384,128]{1,0:T(8,128)} fusion(bf16[16,1024,384]{2,1,0:T(8,128)(2,1)} %bitcast.7, bf16[16,1024,128]{2,1,0:T(8,128)(2,1)} %all-gather.2.cloned.1.call-done), kind=kOutput, calls=%fused_computation | convolution fusion | flops 1610612736 | bytes 16973824 | tf_op jit(solution)/shard_map/dot_general | solution.py:10
  326.0 0.0 all-reduce.2.cloned.1.call-update
  326.0 61.4 %all-reduce.2.cloned.1.call-done = f32[384,128]{1,0:T(8,128)} async-done(((f32[384,128]{1,0:T(8,128)}), f32[384,128]{1,0:T(8,128)}) %all-reduce.2.cloned.1.call-update) | async-done | bytes 196624 | tf_op jit(solution)/shard_map/psum | solution.py:19
  387.4 0.0 copy-done
  387.5 0.0 copy-done.1
  387.5 0.0 copy-done.2
  387.5 1.5 add_divide_fusion
Async XLA Ops:
  14.3 291.0 %all-to-all-start = ((bf16[16,16,64,384]{3,2,1,0:T(8,128)(2,1)}), bf16[16,16,64,384]{3,2,1,0:T(8,128)(2,1)}, u32[]{:S(2)}, u32[]{:S(2)}) async-start(bf16[16,16,64,384]{3,2,1,0:T(8,128)(2,1)} %stack.2), calls=%async_computation | async-start | bytes 25165824 | tf_op jit(solution)/shard_map/all_to_all | solution.py:12
  26.2 289.9 %all-gather.2.cloned.1.call-start = ((), (), s32[]{:S(2)}) async-start(), calls=%async_computation.1 | async-start | bytes 4718592 | tf_op jit(solution)/shard_map/all_gather | solution.py:9
  27.0 360.5 %all-reduce.2.cloned.1.call-start = ((), (), s32[]{:S(2)}) async-start(), calls=%async_computation.2 | async-start | bytes 393216 | tf_op jit(solution)/shard_map/psum | solution.py:19
  316.1 71.4 %copy-start = (bf16[96,128]{1,0:T(8,128)(2,1)S(1)}, bf16[96,128]{1,0:T(8,128)(2,1)}, u32[]{:S(2)}) copy-start(bf16[96,128]{1,0:T(8,128)(2,1)} %param.7) | copy-start | bytes 73732
  316.1 71.4 %copy-start.1 = (f32[128]{0:T(128)S(1)}, f32[128]{0:T(128)}, u32[]{:S(2)}) copy-start(f32[128]{0:T(128)} %param.9) | copy-start | bytes 1540
  316.1 71.4 %copy-start.2 = (f32[96]{0:T(128)S(1)}, f32[96]{0:T(128)}, u32[]{:S(2)}) copy-start(f32[96]{0:T(128)} %param.8) | copy-start | bytes 1156
Sparse Core Ops, SparseCore 0:
  29.2 58.5 all-gather.1
  326.2 61.2 all-reduce.1
